TPU v7x, 32 devices: a whole 2x2x4 slice. The times are simulated.
32 devices in a mesh: pool: 2 (over x), row: 8 (over z, y), col: 2 (over core).
Axes of the slice: x: 2, y: 2, z: 4, core: 2. Of those that a mesh axis runs over, the one named last changes fastest.
Arguments:
- grad_slots: bfloat16 [48, 256, 14336], P(('pool', 'row'), 'col'), parts along dimension 0, may hold values from -6 to 6
- block_owner: int32 [32], P('pool'), parts along dimension 0, may hold values from 0 to 7, as said below
- factor: bfloat16 [8192, 4096], P(('pool', 'col'), 'row'), parts along dimension 0, may hold values from -0.125 to 0.125
- pattern: int32 [16, 8], P('pool'), parts along dimension 0, may hold values from 0 to 1, as said below
Outputs:
- precond: bfloat16 [8192, 14336], P(('pool', 'col'), 'row'), parts along dimension 0
There are 2 independent parts, one for each index of `pool`. A program takes and returns all parts, laid end to end along the dimension named above; each array names one. Nothing has to cross between parts.
Inputs may be any that keep to these rules, and one draw needn't show every extreme that they name: `block_owner`: no trainer shard holds more than 3 blocks and one holds exactly 3; a shard keeps its blocks in its first slots in increasing block order, and the other slots are unused. `pattern`: 1 on the diagonal and 0 below it.
All inputs are finite; a program needn't handle non-finite values.
Results may differ from a plain program's by a relative error of at most 0.004.
Values may be sent and summed in bfloat16 or wider, within the bound.
A program may use at most 192 MiB of HBM per device.

v0:
```python
import jax
import jax.numpy as jnp
from jax import lax
from jax.sharding import PartitionSpec as P


def body(grad_slots, block_owner, factor, pattern):
    row_idx = lax.axis_index("row")
    col_idx = lax.axis_index("col")
    slot_cap = grad_slots.shape[0]
    block_total = block_owner.shape[0]
    received = lax.all_to_all(grad_slots, "row", split_axis=2, concat_axis=0, tiled=True)
    same_owner = block_owner[:, None] == block_owner[None, :]
    earlier = jnp.arange(block_total)[None, :] < jnp.arange(block_total)[:, None]
    owner_rank = jnp.sum(same_owner & earlier, axis=1)
    slot_of = block_owner * slot_cap + owner_rank
    picked = jnp.take(received, slot_of, axis=0)
    blocks = lax.all_gather(picked, "col", axis=1, tiled=True)
    grad_cols = blocks.reshape(-1, blocks.shape[2])
    half_rows, piece_width = factor.shape
    block_count = pattern.shape[0]
    total_rows = 2 * half_rows
    block_size = total_rows // block_count
    half_blocks = block_count // 2
    col_block = (row_idx * piece_width + jnp.arange(piece_width)) // block_size
    row_blocks = col_idx * half_blocks + jnp.arange(half_blocks)
    sel_cols = (jnp.arange(block_count)[:, None] == col_block[None, :]).astype(jnp.float32)
    pattern_cols = jnp.dot(pattern.astype(jnp.float32), sel_cols)
    sel_rows = (row_blocks[:, None] == jnp.arange(block_count)[None, :]).astype(jnp.float32)
    block_mask = jnp.dot(sel_rows, pattern_cols)
    keep_mask = block_mask > 0.5
    shaped = factor.reshape(half_blocks, block_size, piece_width)
    masked = jnp.where(keep_mask[:, None, :], shaped, jnp.zeros_like(shaped)).reshape(
        half_rows, piece_width
    )
    result = jnp.dot(
        lax.all_gather(masked, "row", axis=1, tiled=True),
        grad_cols,
        preferred_element_type=jnp.float32,
    )
    return result.astype(jnp.bfloat16)


def solution(mesh):
    placed = (
        P(("pool", "row"), "col", None),
        P("pool"),
        P(("pool", "col"), "row"),
        P("pool", None),
    )
    return jax.shard_map(
        body, mesh=mesh, in_specs=placed, out_specs=P(("pool", "col"), "row"), check_vma=False
    )
```

profile of v0, /device:TPU:0, one launch (start us, length us, event | category | flops | bytes accessed | tf_op | source)
XLA Modules:
  0.0 657.5 jit_solution(4763586861439865328)
XLA Ops:
  6.5 0.0 all-gather.3.cloned.1.call-start
  6.6 0.9 fusion.3
  7.5 3.1 bitcast_select_fusion
  10.6 0.0 all-gather.3.cloned.1.call-update
  10.6 22.4 %copy.10 = bf16[3,128,14336]{1,0,2:T(4,128)(2,1)} copy(bf16[3,128,14336]{2,1,0:T(8,128)(2,1)} %param.4) | data formatting | bytes 22020096 | tf_op args[0]
  33.0 0.0 copy-start
  33.0 7.4 %all-to-all-start = ((bf16[3,128,14336]{1,0,2:T(4,128)(2,1)}), bf16[3,128,14336]{1,0,2:T(4,128)(2,1)}, u32[]{:S(2)}, u32[]{:S(2)}) async-start(bf16[3,128,14336]{1,0,2:T(4,128)(2,1)} %copy.10), calls=%async_computation | async-start | bytes 29360128 | tf_op jit(solution)/shard_map/all_to_all | solution.py:12
  40.4 0.0 all-gather.5.cloned.1.call-start
  40.5 0.0 copy-done
  40.5 0.2 convert_reduce_fusion
  40.7 504.1 %all-to-all-done = bf16[3,128,14336]{1,0,2:T(4,128)(2,1)} async-done(((bf16[3,128,14336]{1,0,2:T(4,128)(2,1)}), bf16[3,128,14336]{1,0,2:T(4,128)(2,1)}, u32[]{:S(2)}, u32[]{:S(2)}) %all-to-all-start) | async-done | bytes 11010080 | tf_op jit(solution)/shard_map/all_to_all | solution.py:12
  544.8 12.4 %copy.11 = bf16[3,128,14336]{1,2,0:T(8,128)(2,1)} copy(bf16[3,128,14336]{1,0,2:T(4,128)(2,1)} %all-to-all-done) | data formatting | bytes 22020096 | tf_op jit(solution)/shard_map/all_to_all | solution.py:12
  557.2 14.2 %copy.12 = bf16[8,3,128,1792]{3,2,1,0:T(8,128)(2,1)} copy(bf16[8,3,128,1792]{2,3,0,1:T(8,128)(2,1)} %bitcast.9) | data formatting | bytes 22020096 | tf_op jit(solution)/shard_map/all_to_all | solution.py:12
  571.3 8.2 %gather_fusion = bf16[16,128,1792]{2,1,0:T(8,128)(2,1)} fusion(bf16[24,128,1792]{2,1,0:T(8,128)(2,1)} %bitcast.10, s32[1024]{0:T(1024)S(1)} %pad_clamp_fusion), kind=kCustom, calls=%fused_computation | custom fusion | bytes 14680128 | tf_op jit(solution)/shard_map/jit(_take)/gather | solution.py:17
  579.5 6.9 %broadcast_select_fusion = bf16[16,128,1792]{2,1,0:T(8,128)(2,1)} fusion(bf16[16,128,1792]{2,1,0:T(8,128)(2,1)} %gather_fusion, pred[16]{0:T(512)(128)(4,1)S(1)} %get-tuple-element.5), kind=kLoop, calls=%fused_computation.2 | loop fusion | flops 3670016 | bytes 14680080 | tf_op jit(solution)/shard_map/jit(_take)/select_n | solution.py:17
  586.4 0.0 all-gather.5.cloned.1.call-update
  586.5 0.0 all-gather.3.cloned.1.call-done
  586.5 25.5 %all-gather.5.cloned.1.call-done = bf16[16,256,1792]{2,1,0:T(8,128)(2,1)} async-done(((bf16[16,128,1792]{2,1,0:T(8,128)(2,1)}), bf16[16,256,1792]{2,1,0:T(8,128)(2,1)}) %all-gather.5.cloned.1.call-update) | async-done | bytes 14680080 | tf_op jit(solution)/shard_map/all_gather | solution.py:18
  612.0 38.6 %convolution_convert_fusion = bf16[2048,1792]{1,0:T(8,128)(2,1)} fusion(bf16[2048,4096]{1,0:T(8,128)(2,1)} %all-gather.3.cloned.1.call-done, bf16[4096,1792]{1,0:T(8,128)(2,1)} %bitcast.11), kind=kOutput, calls=%fused_computation.1 | convolution fusion | flops 30068441088 | bytes 38797312 | tf_op jit(solution)/shard_map/dot_general | solution.py:36
  (4 shorter events, 0.0 us)
Async XLA Ops:
  6.5 579.9 %all-gather.3.cloned.1.call-start = ((), (), s32[]{:S(2)}) async-start(), calls=%async_computation.1 | async-start | bytes 18874368 | tf_op jit(solution)/shard_map/all_gather | solution.py:37
  33.0 7.5 %copy-start = (s32[16]{0:T(128)S(1)}, s32[16]{0:T(128)}, u32[]{:S(2)}) copy-start(s32[16]{0:T(128)} %param.5) | copy-start | bytes 196
  33.0 511.8 %all-to-all-start = ((bf16[3,128,14336]{1,0,2:T(4,128)(2,1)}), bf16[3,128,14336]{1,0,2:T(4,128)(2,1)}, u32[]{:S(2)}, u32[]{:S(2)}) async-start(bf16[3,128,14336]{1,0,2:T(4,128)(2,1)} %copy.10), calls=%async_computation | async-start | bytes 29360128 | tf_op jit(solution)/shard_map/all_to_all | solution.py:12
  40.4 571.6 %all-gather.5.cloned.1.call-start = ((), (), s32[]{:S(2)}) async-start(), calls=%async_computation.2 | async-start | bytes 22020096 | tf_op jit(solution)/shard_map/all_gather | solution.py:18
Sparse Core Ops, SparseCore 0:
  10.7 526.6 all-gather.2
  586.6 25.3 all-gather.4
where the time goes:
time: 659 us; the launch traced here: 657 us
  waiting for transfers between devices  530 us (80%)
  local copies, waits for them, and re-layouts  57.2 us (9%)
  matrix products  39.5 us (6%)
  between operations  13.4 us (2%)
  other arithmetic  10.2 us (2%)
  starting transfers between devices  7.44 us (1%)
    all_to_all x1, waiting for transfers between devices, body(): lax.all_to_all(grad_slots, 'row', split_axis=2, concat_axis=0, tiled=True)  504 us
    dot_general x1, matrix products, body(): jnp.dot(lax.all_gather(masked, 'row', axis=1, tiled=True), grad_cols, pre...  38.6 us
    all_to_all x2, local copies, waits for them, and re-layouts, body(): lax.all_to_all(grad_slots, 'row', split_axis=2, concat_axis=0, tiled=True)  26.6 us
    all_gather x1, waiting for transfers between devices, body(): blocks = lax.all_gather(picked, 'col', axis=1, tiled=True)  25.5 us
    unnamed x3, local copies, waits for them, and re-layouts  22.4 us
  transfers between devices with their start and end apart: 3, of which 2 were waited for; matrix products, arithmetic and copies ran while one was open for 10% of the time, Pallas kernels for 0%

commit v1 on v0

--- a/solution.py
+++ b/solution.py
@@ -9,7 +9,19 @@
     col_idx = lax.axis_index("col")
     slot_cap = grad_slots.shape[0]
     block_total = block_owner.shape[0]
-    received = lax.all_to_all(grad_slots, "row", split_axis=2, concat_axis=0, tiled=True)
+    ways, here = (lax.axis_size("row"), lax.axis_index("row"))
+    width = grad_slots.shape[2] // ways
+    dims = list(grad_slots.shape)
+    dims[2] = width
+    height = dims[0]
+    dims[0] = height * ways
+    full = jnp.zeros(dims, grad_slots.dtype)
+    for mask in range(ways):
+        part = lax.dynamic_slice_in_dim(grad_slots, (here ^ mask) * width, width, axis=2)
+        if mask:
+            part = lax.ppermute(part, "row", [(d, d ^ mask) for d in range(ways)])
+        full = lax.dynamic_update_slice_in_dim(full, part, (here ^ mask) * height, axis=0)
+    received = full
     same_owner = block_owner[:, None] == block_owner[None, :]
     earlier = jnp.arange(block_total)[None, :] < jnp.arange(block_total)[:, None]
     owner_rank = jnp.sum(same_owner & earlier, axis=1)

time: 659 us -> 585 us (0.89)
  waiting for transfers between devices: 530 us -> 474 us
  local copies, waits for them, and re-layouts: 57.2 us -> 35.4 us
    all_to_all x1 -> x0, waiting for transfers between devices: 504 us -> none  [body(): lax.all_to_all(grad_slots, 'row', split_axis=2, concat_axis=0, tiled=True)]
    all_gather x1, waiting for transfers between devices: 0.02 us -> 231 us  [body(): lax.all_gather(masked, 'row', axis=1, tiled=True)]
    ppermute x0 -> x7, waiting for transfers between devices: none -> 165 us  [body(): part = lax.ppermute(part, 'row', [(d, d ^ mask) for d in range(ways)])]
    all_gather x1, waiting for transfers between devices: 25.5 us -> 78.1 us  [body(): blocks = lax.all_gather(picked, 'col', axis=1, tiled=True)]
    all_to_all x2 -> x0, local copies, waits for them, and re-layouts: 26.6 us -> none  [body(): lax.all_to_all(grad_slots, 'row', split_axis=2, concat_axis=0, tiled=True)]
    unnamed x3 -> x6, local copies, waits for them, and re-layouts: 22.4 us -> 1.08 us
    ppermute x0 -> x7, starting transfers between devices: none -> 13.6 us  [body(): part = lax.ppermute(part, 'row', [(d, d ^ mask) for d in range(ways)])]
    dynamic_update_slice x0 -> x7, local copies, waits for them, and re-layouts: none -> 12.4 us  [body(): lax.dynamic_update_slice_in_dim(full, part, (here ^ mask) * height, axis=0)]
  transfers between devices with their start and end apart: 3 -> 9, of which waited for: 2 -> 6; matrix products, arithmetic and copies ran while one was open for 10% -> 2% of each run, Pallas kernels for 0% -> 0%
where the time goes in v1:
time: 585 us; the launch traced here: 584 us
  waiting for transfers between devices  474 us (81%)
  matrix products  39 us (7%)
  local copies, waits for them, and re-layouts  35.4 us (6%)
  starting transfers between devices  13.7 us (2%)
  between operations  13.4 us (2%)
  other arithmetic  8.56 us (1%)
    all_gather x1, waiting for transfers between devices, body(): lax.all_gather(masked, 'row', axis=1, tiled=True)  231 us
    ppermute x7, waiting for transfers between devices, body(): part = lax.ppermute(part, 'row', [(d, d ^ mask) for d in range(ways)])  165 us
    all_gather x1, waiting for transfers between devices, body(): blocks = lax.all_gather(picked, 'col', axis=1, tiled=True)  78.1 us
    dot_general x1, matrix products, body(): jnp.dot(lax.all_gather(masked, 'row', axis=1, tiled=True), grad_cols, pre...  38.6 us
    ppermute x7, starting transfers between devices, body(): part = lax.ppermute(part, 'row', [(d, d ^ mask) for d in range(ways)])  13.6 us
    dynamic_update_slice x7, local copies, waits for them, and re-layouts, body(): lax.dynamic_update_slice_in_dim(full, part, (here ^ mask) * height, axis=0)  12.4 us
  transfers between devices with their start and end apart: 9, of which 6 were waited for; matrix products, arithmetic and copies ran while one was open for 2% of the time, Pallas kernels for 0%

profile of v1, /device:TPU:0, one launch (start us, length us, event | category | flops | bytes accessed | tf_op | source)
XLA Modules:
  0.0 584.3 jit_solution(2557090740590469201)
XLA Ops:
  6.5 0.0 all-gather.5.cloned.1.call-start
  6.5 5.4 broadcast_in_dim.41
  11.9 0.0 copy-start.1
  11.9 8.4 %constant_dynamic-slice_fusion = (bf16[3,128,1792]{2,1,0:T(8,128)(2,1)}, bf16[3,128,1792]{2,1,0:T(8,128)(2,1)}, bf16[3,128,1792]{2,1,0:T(8,128)(2,1)}, bf16[3,12...) fusion(bf16[3,128,14336]{2,1,0:T(8,128)(2,1)} %param.4, ...), kind=kLoop, calls=%fused_computation.16 | loop fusion | bytes 22020132 | tf_op jit(solution)/shard_map/dynamic_slice | solution.py:20
  20.3 3.0 collective-permute-start
  23.3 1.6 collective-permute-start.1
  24.9 0.0 collective-permute-start.2
  24.9 3.0 collective-permute-start.3
  27.9 1.3 collective-permute-start.4
  29.2 0.0 copy-done.1
  29.2 0.2 convert_reduce_fusion
  29.3 24.4 %collective-permute-done = bf16[3,128,1792]{2,1,0:T(8,128)(2,1)} collective-permute-done((bf16[3,128,1792]{2,1,0:T(8,128)(2,1)}, bf16[3,128,1792]{2,1,0:T(8,128)(2,1)}, u32[]{:S(2)}, u32[]{:S(2)}) %collective-permute-start) | collective-permute-done | bytes 1376288 | tf_op jit(solution)/shard_map/ppermute | solution.py:22
  53.8 3.8 collective-permute-start.5
  57.6 57.1 %collective-permute-done.1 = bf16[3,128,1792]{2,1,0:T(8,128)(2,1)} collective-permute-done((bf16[3,128,1792]{2,1,0:T(8,128)(2,1)}, bf16[3,128,1792]{2,1,0:T(8,128)(2,1)}, u32[]{:S(2)}, u32[]{:S(2)}) %collective-permute-start.1) | collective-permute-done | bytes 1376288 | tf_op jit(solution)/shard_map/ppermute | solution.py:22
  114.8 1.0 collective-permute-start.6
  115.8 2.5 constant_dynamic-update-slice_fusion.5
  118.3 2.5 constant_dynamic-update-slice_fusion.4
  120.8 21.1 %collective-permute-done.2 = bf16[3,128,1792]{2,1,0:T(8,128)(2,1)} collective-permute-done((bf16[3,128,1792]{2,1,0:T(8,128)(2,1)}, bf16[3,128,1792]{2,1,0:T(8,128)(2,1)}, u32[]{:S(2)}, u32[]{:S(2)}) %collective-permute-start.2) | collective-permute-done | bytes 1376288 | tf_op jit(solution)/shard_map/ppermute | solution.py:22
  141.9 2.5 constant_dynamic-update-slice_fusion.3
  144.4 0.0 collective-permute-done.3
  144.4 1.2 constant_dynamic-update-slice_fusion.2
  145.6 62.3 %collective-permute-done.4 = bf16[3,128,1792]{2,1,0:T(8,128)(2,1)S(1)} collective-permute-done((bf16[3,128,1792]{2,1,0:T(8,128)(2,1)}, bf16[3,128,1792]{2,1,0:T(8,128)(2,1)S(1)}, u32[]{:S(2)}, u32[]{:S(2)}) %collective-permute-start.4) | collective-permute-done | bytes 1376288 | tf_op jit(solution)/shard_map/ppermute | solution.py:22
  207.9 1.2 constant_dynamic-update-slice_fusion.1
  209.1 0.0 collective-permute-done.5
  209.1 1.3 constant_dynamic-update-slice_fusion
  210.4 0.0 collective-permute-done.6
  210.4 1.2 constant_dynamic-update-slice_fusion.6
  211.5 8.2 %gather_fusion = bf16[16,128,1792]{2,1,0:T(8,128)(2,1)} fusion(bf16[24,128,1792]{2,1,0:T(8,128)(2,1)} %constant_dynamic-update-slice_fusion.6, s32[1024]{0:T(1024)S(1)} %pad_clamp_fusion), kind=kCustom, calls=%fused_computation | custom fusion | bytes 14680128 | tf_op jit(solution)/shard_map/jit(_take)/gather | solution.py:29
  219.7 6.9 %broadcast_select_fusion = bf16[16,128,1792]{2,1,0:T(8,128)(2,1)} fusion(bf16[16,128,1792]{2,1,0:T(8,128)(2,1)} %gather_fusion, pred[16]{0:T(512)(128)(4,1)S(1)} %get-tuple-element.5), kind=kLoop, calls=%fused_computation.2 | loop fusion | flops 3670016 | bytes 14680080 | tf_op jit(solution)/shard_map/jit(_take)/select_n | solution.py:29
  226.6 0.0 copy-start.2
  226.6 0.0 copy-start
  226.6 0.0 all-gather.5.cloned.1.call-update
  226.7 0.0 all-gather.3.cloned.1.call-start
  226.8 0.6 copy-done.2
  227.3 0.4 fusion.3
  227.7 0.5 copy-done
  228.2 1.4 bitcast_select_fusion
  229.7 0.0 all-gather.3.cloned.1.call-update
  229.7 78.1 %all-gather.5.cloned.1.call-done = bf16[16,256,1792]{2,1,0:T(8,128)(2,1)} async-done(((bf16[16,128,1792]{2,1,0:T(8,128)(2,1)}), bf16[16,256,1792]{2,1,0:T(8,128)(2,1)}) %all-gather.5.cloned.1.call-update) | async-done | bytes 14680080 | tf_op jit(solution)/shard_map/all_gather | solution.py:30
  307.8 231.0 %all-gather.3.cloned.1.call-done = bf16[2048,4096]{1,0:T(8,128)(2,1)} async-done(((bf16[2048,512]{1,0:T(8,128)(2,1)}), bf16[2048,4096]{1,0:T(8,128)(2,1)}) %all-gather.3.cloned.1.call-update) | async-done | bytes 16777232 | tf_op jit(solution)/shard_map/all_gather | solution.py:49
  538.8 38.6 %convolution_convert_fusion = bf16[2048,1792]{1,0:T(8,128)(2,1)} fusion(bf16[2048,4096]{1,0:T(8,128)(2,1)} %all-gather.3.cloned.1.call-done, bf16[4096,1792]{1,0:T(8,128)(2,1)} %bitcast.5), kind=kOutput, calls=%fused_computation.1 | convolution fusion | flops 30068441088 | bytes 38797312 | tf_op jit(solution)/shard_map/dot_general | solution.py:48
  (4 shorter events, 0.0 us)
Async XLA Ops:
  6.5 301.3 %all-gather.5.cloned.1.call-start = ((), (), s32[]{:S(2)}) async-start(), calls=%async_computation.1 | async-start | bytes 22020096 | tf_op jit(solution)/shard_map/all_gather | solution.py:30
  11.9 17.3 %copy-start.1 = (s32[16]{0:T(128)S(1)}, s32[16]{0:T(128)}, u32[]{:S(2)}) copy-start(s32[16]{0:T(128)} %param.5) | copy-start | bytes 196
  20.3 33.5 %collective-permute-start = (bf16[3,128,1792]{2,1,0:T(8,128)(2,1)}, bf16[3,128,1792]{2,1,0:T(8,128)(2,1)}, u32[]{:S(2)}, u32[]{:S(2)}) collective-permute-start(bf16[3,128,1792]{2,1,0:T(8,128)(2,1)} %get-tuple-element.12), channel_id=1, source_target_pairs={{0,2},{2,0},{4,6},{6,4},{8,10},{10,8},{12,14},{14,12},{1,3},{3,1},... | collective-permute-start | bytes 4128776 | tf_op jit(solution)/shard_map/ppermute | solution.py:22
  23.3 91.5 %collective-permute-start.1 = (bf16[3,128,1792]{2,1,0:T(8,128)(2,1)}, bf16[3,128,1792]{2,1,0:T(8,128)(2,1)}, u32[]{:S(2)}, u32[]{:S(2)}) collective-permute-start(bf16[3,128,1792]{2,1,0:T(8,128)(2,1)} %get-tuple-element.11), channel_id=1, source_target_pairs={{0,4},{2,6},{4,0},{6,2},{8,12},{10,14},{12,8},{14,10},{1,5},{3,7},... | collective-permute-start | bytes 4128776 | tf_op jit(solution)/shard_map/ppermute | solution.py:22
  24.9 117.0 %collective-permute-start.2 = (bf16[3,128,1792]{2,1,0:T(8,128)(2,1)}, bf16[3,128,1792]{2,1,0:T(8,128)(2,1)}, u32[]{:S(2)}, u32[]{:S(2)}) collective-permute-start(bf16[3,128,1792]{2,1,0:T(8,128)(2,1)} %get-tuple-element.10), channel_id=1, source_target_pairs={{0,6},{2,4},{4,2},{6,0},{8,14},{10,12},{12,10},{14,8},{1,7},{3,5},... | collective-permute-start | bytes 4128776 | tf_op jit(solution)/shard_map/ppermute | solution.py:22
  24.9 119.6 %collective-permute-start.3 = (bf16[3,128,1792]{2,1,0:T(8,128)(2,1)}, bf16[3,128,1792]{2,1,0:T(8,128)(2,1)S(1)}, u32[]{:S(2)}, u32[]{:S(2)}) collective-permute-start(bf16[3,128,1792]{2,1,0:T(8,128)(2,1)} %get-tuple-element.9), channel_id=1, source_target_pairs={{0,8},{2,10},{4,12},{6,14},{8,0},{10,2},{12,4},{14,6},{1,9},{3,11}... | collective-permute-start | bytes 4128776 | tf_op jit(solution)/shard_map/ppermute | solution.py:22
  27.9 180.1 %collective-permute-start.4 = (bf16[3,128,1792]{2,1,0:T(8,128)(2,1)}, bf16[3,128,1792]{2,1,0:T(8,128)(2,1)S(1)}, u32[]{:S(2)}, u32[]{:S(2)}) collective-permute-start(bf16[3,128,1792]{2,1,0:T(8,128)(2,1)} %get-tuple-element.8), channel_id=1, source_target_pairs={{0,10},{2,8},{4,14},{6,12},{8,2},{10,0},{12,6},{14,4},{1,11},{3,9}... | collective-permute-start | bytes 4128776 | tf_op jit(solution)/shard_map/ppermute | solution.py:22
  53.8 155.3 %collective-permute-start.5 = (bf16[3,128,1792]{2,1,0:T(8,128)(2,1)}, bf16[3,128,1792]{2,1,0:T(8,128)(2,1)S(1)}, u32[]{:S(2)}, u32[]{:S(2)}) collective-permute-start(bf16[3,128,1792]{2,1,0:T(8,128)(2,1)} %get-tuple-element.14), channel_id=1, source_target_pairs={{0,12},{2,14},{4,8},{6,10},{8,4},{10,6},{12,0},{14,2},{1,13},{3,15... | collective-permute-start | bytes 4128776 | tf_op jit(solution)/shard_map/ppermute | solution.py:22
  114.8 95.6 %collective-permute-start.6 = (bf16[3,128,1792]{2,1,0:T(8,128)(2,1)}, bf16[3,128,1792]{2,1,0:T(8,128)(2,1)S(1)}, u32[]{:S(2)}, u32[]{:S(2)}) collective-permute-start(bf16[3,128,1792]{2,1,0:T(8,128)(2,1)} %get-tuple-element.7), channel_id=1, source_target_pairs={{0,14},{2,12},{4,10},{6,8},{8,6},{10,4},{12,2},{14,0},{1,15},{3,13... | collective-permute-start | bytes 4128776 | tf_op jit(solution)/shard_map/ppermute | solution.py:22
  226.6 0.7 copy-start.2
  226.6 1.6 copy-start
  226.7 312.1 %all-gather.3.cloned.1.call-start = ((), (), s32[]{:S(2)}) async-start(), calls=%async_computation | async-start | bytes 18874368 | tf_op jit(solution)/shard_map/all_gather | solution.py:49
Sparse Core Ops, SparseCore 0:
  226.8 80.9 all-gather.4
  309.9 228.9 all-gather.2
